TPU v7x, 256 devices: a whole 4x4x8 slice. The times are simulated.
256 devices in a mesh: row: 8 (over z), col: 8 (over y, core), depth: 4 (over x).
Axes of the slice: x: 4, y: 4, z: 8, core: 2. Of those that a mesh axis runs over, the one named last changes fastest.
Arguments:
- p_blocks: bfloat16 [256, 64, 16384], P('row', None, 'col'), may hold values from -0.25 to 0.25
- p_cols: int32 [256, 256], P('row', 'col'), may hold values from -1 to 255, as said below
- out_mask: int32 [256, 8], P(('row', 'col', 'depth')), may hold values 0 or 1
Outputs:
- purified: float32 [256, 64, 512], P(('row', 'col', 'depth'))
Inputs may be any that keep to these rules, and one draw needn't show every extreme that they name: `p_cols`: slot c * 32 + s of a block row holds a block column of c * 32 to (c + 1) * 32 - 1 or -1; the column numbers of a block row are distinct; within each group of 32 slots the used slots come first and at least one is used; in the group that holds a block row's own block column all 32 slots are used.
All inputs are finite; a program needn't handle non-finite values. No bound on the sum of `out_mask` on one device may be relied on, other than what follows from the above.
Results may differ from a plain program's by a relative error of at most 0.0027.
Values may be sent and summed in bfloat16 or wider, within the bound.
A program may use at most 128 MiB of HBM per device.

v0:
```python
import jax
import jax.numpy as jnp
from jax import lax
from jax.sharding import PartitionSpec as P


def from_root(value, axis, source):
    kept = jnp.where(lax.axis_index(axis) == source, value, 0).astype(value.dtype)
    return lax.psum(kept, axis)


def group_of():
    return 4


def expand_index(block_ids, block_size):
    offsets = jnp.arange(block_size, dtype=jnp.int32)
    return (block_ids[:, :, None] * block_size + offsets[None, None, :]).reshape(
        block_ids.shape[0], -1
    )


def sparse_product(used_blocks, local_ids, panel_rows, block_size):
    row_count = used_blocks.shape[0]
    slot_count = local_ids.shape[1]
    width = panel_rows.shape[1]
    group = group_of()

    def advance(turn, total):
        blocks_now = lax.dynamic_slice_in_dim(
            used_blocks, turn * group * block_size, group * block_size, 2
        )
        ids_now = lax.dynamic_slice_in_dim(local_ids, turn * group, group, 1)
        picked = jnp.take(panel_rows, expand_index(ids_now, block_size), axis=0)
        return total + jnp.einsum(
            "iak,ikn->ian", blocks_now, picked, preferred_element_type=jnp.float32
        )

    start_total = jnp.zeros((row_count, block_size, width), jnp.float32)
    return lax.fori_loop(0, slot_count // group, advance, start_total)


def densify(p_blocks, p_cols, first_col, count, block_size):
    row_count = p_blocks.shape[0]
    slot_count = p_cols.shape[1]
    targets = first_col + jnp.arange(count, dtype=jnp.int32)
    selector = (p_cols[:, :, None] == targets[None, None, :]).astype(jnp.bfloat16)
    blocks = p_blocks.reshape(row_count, block_size, slot_count, block_size)
    picked = jnp.einsum("iasb,isw->iawb", blocks, selector, preferred_element_type=jnp.float32)
    return picked.astype(jnp.bfloat16).reshape(row_count, block_size, count * block_size)


def body(p_blocks, p_cols, out_mask):
    row_count = p_blocks.shape[0]
    block_size = p_blocks.shape[1]
    slot_count = p_cols.shape[1]
    window = out_mask.shape[1]
    panel_width = window // 2
    row_size = lax.axis_size("row")
    col_size = lax.axis_size("col")
    depth_size = lax.axis_size("depth")
    col_index = lax.axis_index("col")
    depth_index = lax.axis_index("depth")
    group_cols = row_count * row_size // col_size
    half_start = row_count * row_size // 2
    ratio = row_size // col_size
    used_slot = p_cols >= 0
    local_ids = jnp.where(used_slot, p_cols - col_index * group_cols, 0)
    used_cols = jnp.repeat(used_slot, block_size, axis=1)
    used_blocks = jnp.where(used_cols[:, None, :], p_blocks, jnp.zeros((), jnp.bfloat16))
    pieces = []
    for panel_id in range(2):
        densified = densify(p_blocks, p_cols, panel_id * half_start, panel_width, block_size)
        pieces.append(from_root(densified, "col", panel_id * (col_size // 2)))
    panel_block = jnp.concatenate(pieces, axis=2)
    piece_id = 0
    received = from_root(panel_block, "row", col_index * ratio + piece_id)
    panel_rows = received.reshape(-1, panel_block.shape[2])
    slot_share = slot_count // depth_size
    depth_blocks = lax.dynamic_slice_in_dim(
        used_blocks, depth_index * slot_share * block_size, slot_share * block_size, 2
    )
    depth_ids = lax.dynamic_slice_in_dim(local_ids, depth_index * slot_share, slot_share, 1)
    first_terms = sparse_product(depth_blocks, depth_ids, panel_rows, block_size)
    square = lax.psum_scatter(first_terms, ("col", "depth"), scatter_dimension=0, tiled=True)
    square_block = lax.all_gather(square.astype(jnp.bfloat16), ("col", "depth"), axis=0, tiled=True)
    piece_id = 0
    received_square = from_root(square_block, "row", col_index * ratio + piece_id)
    square_rows = received_square.reshape(-1, square_block.shape[2])
    second_terms = sparse_product(depth_blocks, depth_ids, square_rows, block_size)
    cube = lax.psum_scatter(second_terms, ("col", "depth"), scatter_dimension=0, tiled=True)
    result = 3.0 * square - 2.0 * cube
    out_rows = result.shape[0]
    shaped = result.reshape(out_rows, block_size, window, block_size)
    shaped = shaped * out_mask.astype(jnp.float32)[:, None, :, None]
    return shaped.reshape(out_rows, block_size, window * block_size)


def solution(mesh):
    in_specs = (P("row", None, "col"), P("row", "col"), P(("row", "col", "depth"), None))
    out_specs = P(("row", "col", "depth"), None, None)
    return jax.shard_map(body, mesh=mesh, in_specs=in_specs, out_specs=out_specs, check_vma=False)
```

profile of v0, /device:TPU:1, one launch (start us, length us, event | category | flops | bytes accessed | tf_op | source)
XLA Modules:
  0.0 701.4 jit_solution(13752102514315627002)
XLA Ops:
  6.5 24.4 %reshape.72 = bf16[32,64,32,64]{3,2,1,0:T(8,128)(2,1)} reshape(bf16[32,64,2048]{2,1,0:T(8,128)(2,1)} %param.9) | data formatting | bytes 16777216 | tf_op jit(solution)/shard_map/reshape | solution.py:48
  31.0 8.1 %select_bitcast_fusion = bf16[32,64,4,64]{3,2,1,0:T(4,128)(2,1)S(1)} fusion(pred[]{:T(512)S(6)} %eq.39, bf16[32,64,32,64]{3,2,1,0:T(8,128)(2,1)} %reshape.72, s32[32,32]{1,0:T(8,128)S(1)} %copy-done.1, s32[4]{0:T(128)S(1)} %iota_add_fusion), kind=kOutput, calls=%fused_computation.30 | convolution fusion | flops 34607104 | bytes 9441297 | tf_op jit(solution)/shard_map/iasb,isw->iawb/dot_general | solution.py:49
  39.1 2.1 select_n.111
  41.2 8.1 %select_bitcast_fusion.1 = bf16[32,64,4,64]{3,2,1,0:T(4,128)(2,1)S(1)} fusion(pred[]{:T(512)S(6)} %eq.17, bf16[32,64,32,64]{3,2,1,0:T(8,128)(2,1)} %reshape.72, s32[32,32]{1,0:T(8,128)S(1)} %copy-done.1), kind=kOutput, calls=%fused_computation.31 | convolution fusion | flops 34607104 | bytes 9441281 | tf_op jit(solution)/shard_map/iasb,isw->iawb/dot_general | solution.py:49
  49.3 2.1 select_n.107
  51.5 72.9 %all-reduce.9.cloned.1.call-done = (bf16[32,64,256]{2,1,0:T(8,128)(2,1)}, bf16[32,64,256]{2,1,0:T(8,128)(2,1)}) async-done(((bf16[32,64,256]{2,1,0:T(8,128)(2,1)}, bf16[32,64,256]{2,1,0:T(8,128)(2,1)}), (bf16[32,64,256]{2,1,0:T(8,128)(2,1)}, bf16[32,64,256]{2,1,0:T(8,128)(2,1)})) %all-reduce.9.cloned.1.call-update) | async-done | bytes 2097168 | tf_op jit(solution)/shard_map/psum | solution.py:9
  124.4 3.4 maximum_select_fusion
  128.4 2.2 dynamic-slice_select_fusion
  130.6 77.7 %all-reduce.5.cloned.1.call-done = bf16[2048,512]{1,0:T(8,128)(2,1)} async-done(((bf16[2048,512]{1,0:T(8,128)(2,1)}), bf16[2048,512]{1,0:T(8,128)(2,1)}) %all-reduce.5.cloned.1.call-update) | async-done | bytes 2097168 | tf_op jit(solution)/shard_map/psum | solution.py:9
  208.3 85.4 %while.32 = (s32[]{:T(128)}, f32[32,64,512]{2,1,0:T(8,128)}, bf16[32,64,512]{2,1,0:T(8,128)(2,1)S(1)}, s32[32,8]{1,0:T(8,128)S(1)}, bf16[2048,512]{1,0:T(8,128)(...) while((s32[]{:T(128)}, f32[32,64,512]{2,1,0:T(8,128)}, ...), condition=%wide.region_4.6_spmd.clone, body=%wide.region_3.5_spmd.clone.sunk | while | flops 543260800 | bytes 34986712 | solution.py:40
  208.8 35.8 %gather_fusion = bf16[8192,512]{1,0:T(8,128)(2,1)} fusion(bf16[2048,512]{1,0:T(8,128)(2,1)} %get-tuple-element.418, s32[8192]{0:T(1024)S(1)} %broadcast_clamp_fusion.4), kind=kCustom, calls=%fused_computation.clone.clone.1 | custom fusion | bytes 16809984 | tf_op jit(solution)/shard_map/while/body/eval_jaxpr/jit(_take)/gather | solution.py:34
  244.6 5.8 select_add_fusion.4
  250.8 35.8 %gather_fusion = bf16[8192,512]{1,0:T(8,128)(2,1)} fusion(bf16[2048,512]{1,0:T(8,128)(2,1)} %get-tuple-element.418, s32[8192]{0:T(1024)S(1)} %broadcast_clamp_fusion.4), kind=kCustom, calls=%fused_computation.clone.clone.1 | custom fusion | bytes 16809984 | tf_op jit(solution)/shard_map/while/body/eval_jaxpr/jit(_take)/gather | solution.py:34
  286.7 7.0 select_add_fusion.4
  293.8 89.9 %reduce-scatter.3.cloned.1.call-done = f32[1,64,512]{2,1,0:T(8,128)} async-done(((f32[32,64,512]{2,1,0:T(8,128)}), f32[1,64,512]{2,1,0:T(8,128)}) %reduce-scatter.3.cloned.1.call-update) | async-done | bytes 131088 | tf_op jit(solution)/shard_map/reduce_scatter | solution.py:85
  385.3 51.5 %all-gather.2.cloned.1.call-done = bf16[32,64,512]{2,1,0:T(8,128)(2,1)} async-done(((bf16[1,64,512]{2,1,0:T(8,128)(2,1)}), bf16[32,64,512]{2,1,0:T(8,128)(2,1)}) %all-gather.2.cloned.1.call-update) | async-done | bytes 2097168 | tf_op jit(solution)/shard_map/all_gather | solution.py:86
  438.3 79.4 %all-reduce.7.cloned.1.call-done = bf16[2048,512]{1,0:T(8,128)(2,1)} async-done(((bf16[2048,512]{1,0:T(8,128)(2,1)}), bf16[2048,512]{1,0:T(8,128)(2,1)}) %all-reduce.7.cloned.1.call-update) | async-done | bytes 2097168 | tf_op jit(solution)/shard_map/psum | solution.py:9
  517.7 85.4 %while.33 = (s32[]{:T(128)}, f32[32,64,512]{2,1,0:T(8,128)}, bf16[32,64,512]{2,1,0:T(8,128)(2,1)S(1)}, s32[32,8]{1,0:T(8,128)S(1)}, bf16[2048,512]{1,0:T(8,128)(...) while((s32[]{:T(128)}, f32[32,64,512]{2,1,0:T(8,128)}, ...), condition=%wide.region_8.10_spmd.clone, body=%wide.region_7.9_spmd.clone.sunk | while | flops 543260800 | bytes 34986712 | solution.py:40
  518.1 35.8 %gather_fusion.1 = bf16[8192,512]{1,0:T(8,128)(2,1)} fusion(bf16[2048,512]{1,0:T(8,128)(2,1)} %get-tuple-element.451, s32[8192]{0:T(1024)S(1)} %broadcast_clamp_fusion.5), kind=kCustom, calls=%fused_computation.1.clone.clone.1 | custom fusion | bytes 16809984 | tf_op jit(solution)/shard_map/while/body/eval_jaxpr/jit(_take)/gather | solution.py:34
  554.0 5.8 select_add_fusion.5
  560.2 35.8 %gather_fusion.1 = bf16[8192,512]{1,0:T(8,128)(2,1)} fusion(bf16[2048,512]{1,0:T(8,128)(2,1)} %get-tuple-element.451, s32[8192]{0:T(1024)S(1)} %broadcast_clamp_fusion.5), kind=kCustom, calls=%fused_computation.1.clone.clone.1 | custom fusion | bytes 16809984 | tf_op jit(solution)/shard_map/while/body/eval_jaxpr/jit(_take)/gather | solution.py:34
  596.1 7.0 select_add_fusion.5
  603.9 89.1 %reduce-scatter.5.cloned.1.call-done = f32[1,64,512]{2,1,0:T(8,128)} async-done(((f32[32,64,512]{2,1,0:T(8,128)}), f32[1,64,512]{2,1,0:T(8,128)}) %reduce-scatter.5.cloned.1.call-update) | async-done | bytes 131088 | tf_op jit(solution)/shard_map/reduce_scatter | solution.py:91
  693.0 1.6 subtract_multiply_fusion
  (67 shorter events, 6.3 us)
Async XLA Ops:
  6.5 117.9 %all-reduce.9.cloned.1.call-start = ((), (), s32[]{:S(2)}) async-start(), calls=%async_computation.7 | async-start | bytes 4194304 | tf_op jit(solution)/shard_map/psum | solution.py:9
  6.5 24.4 %copy-start.1 = (s32[32,32]{1,0:T(8,128)S(1)}, s32[32,32]{1,0:T(8,128)}, u32[]{:S(2)}) copy-start(s32[32,32]{1,0:T(8,128)} %param.10) | copy-start | bytes 12292
  51.5 156.9 %all-reduce.5.cloned.1.call-start = ((), (), s32[]{:S(2)}) async-start(), calls=%async_computation.2 | async-start | bytes 4194304 | tf_op jit(solution)/shard_map/psum | solution.py:9
  127.8 255.9 %reduce-scatter.3.cloned.1.call-start = ((), (), s32[]{:S(2)}) async-start(), calls=%async_computation.3 | async-start | bytes 4325376 | tf_op jit(solution)/shard_map/reduce_scatter | solution.py:85
  293.8 143.0 %all-gather.2.cloned.1.call-start = ((), (), s32[]{:S(2)}) async-start(), calls=%async_computation.4 | async-start | bytes 2162688 | tf_op jit(solution)/shard_map/all_gather | solution.py:86
  385.2 132.5 %all-reduce.7.cloned.1.call-start = ((), (), s32[]{:S(2)}) async-start(), calls=%async_computation.5 | async-start | bytes 4194304 | tf_op jit(solution)/shard_map/psum | solution.py:9
  438.2 254.8 %reduce-scatter.5.cloned.1.call-start = ((), (), s32[]{:S(2)}) async-start(), calls=%async_computation.6 | async-start | bytes 4325376 | tf_op jit(solution)/shard_map/reduce_scatter | solution.py:91
  603.1 0.7 copy-start.2
  603.1 89.9 %copy-start = (f32[1,64,512]{2,1,0:T(8,128)S(1)}, f32[1,64,512]{2,1,0:T(8,128)}, u32[]{:S(2)}) copy-start(f32[1,64,512]{2,1,0:T(8,128)} %reduce-scatter.3.cloned.1.call-done) | copy-start | bytes 393220
Sparse Core Ops, SparseCore 0:
  51.6 72.7 all-reduce.8
  127.9 80.3 all-reduce.4
  293.9 89.7 reduce-scatter.2
  386.4 50.2 all-gather.1
  439.1 78.6 all-reduce.6
  603.3 89.7 reduce-scatter.4
where the time goes:
time: 703 us; the launch traced here: 701 us
  waiting for transfers between devices  461 us (66%)
  local copies, waits for them, and re-layouts  175 us (25%)
  matrix products  41.8 us (6%)
  between operations  13.6 us (2%)
  other arithmetic  10.6 us (2%)
    psum x3, waiting for transfers between devices, from_root(): return lax.psum(kept, axis)  230 us
    gather x4, local copies, waits for them, and re-layouts, advance(): picked = jnp.take(panel_rows, expand_index(ids_now, block_size), axis=0)  143 us
    reduce_scatter x1, waiting for transfers between devices, body(): lax.psum_scatter(first_terms, ('col', 'depth'), scatter_dimension=0, tile...  89.9 us
    reduce_scatter x1, waiting for transfers between devices, body(): lax.psum_scatter(second_terms, ('col', 'depth'), scatter_dimension=0, til...  89.1 us
    all_gather x1, waiting for transfers between devices, body(): lax.all_gather(square.astype(jnp.bfloat16), ('col', 'depth'), axis=0, til...  51.5 us
    dot_general x4, matrix products, advance(): jnp.einsum('iak,ikn->ian', blocks_now, picked, preferred_element_type=jnp...  25.6 us
    reshape x1, local copies, waits for them, and re-layouts, densify(): blocks = p_blocks.reshape(row_count, block_size, slot_count, block_size)  24.4 us
    dot_general x2, matrix products, densify(): jnp.einsum('iasb,isw->iawb', blocks, selector, preferred_element_type=jnp...  16.2 us
  transfers between devices with their start and end apart: 6, of which 6 were waited for; matrix products, arithmetic and copies ran while one was open for 0% of the time, Pallas kernels for 0%

commit v1 on v0

v1 whole, which is shorter than its diff:
```python
import functools

import jax
import jax.numpy as jnp
from jax import lax
from jax.experimental import pallas as pl
from jax.experimental.pallas import tpu as pltpu
from jax.sharding import PartitionSpec as P

MESH = pl.DeviceIdType.MESH
LANES = 128


def kernel(
    R, C, D, RB, BS, WB,
    p_hbm, codes, out,
    p, dense, panel, x1, x2, part, recv, square, rounded, cubes, owned,
    load_sem, scat_send, scat_recv, ag1_send, ag1_recv, rs_send, rs_recv,
    ag2_send, ag2_recv, sq_send, sq_recv, cu_send, cu_recv,
):
    r, c, d = lax.axis_index("row"), lax.axis_index("col"), lax.axis_index("depth")
    PB = RB // C
    PR = PB * BS
    K = RB * BS
    T = K // LANES
    half = D // 2
    cs = (d // half) * (C // 2)
    window = d % half

    def remote(src, dst, ss, rs, did):
        return pltpu.make_async_remote_copy(
            src_ref=src, dst_ref=dst, send_sem=ss, recv_sem=rs,
            device_id=did, device_id_type=MESH)

    def load(t):
        return pltpu.make_async_copy(
            p_hbm.at[:, :, pl.ds(t * LANES, LANES)], p.at[pl.ds(t * RB, RB)], load_sem.at[t])

    for t in range(T):
        load(t).start()

    barrier = pltpu.get_barrier_semaphore()

    def hello(did):
        pl.semaphore_signal(barrier, inc=1, device_id=did, device_id_type=MESH)

    for k in range(1, R):
        hello((lax.rem(r + k, R), c, d))
    for k in range(C):
        for e in range(D):
            if k or e:
                hello((r, lax.rem(c + k, C), lax.rem(d + e, D)))
    for k in range(R):
        @pl.when((lax.rem(r + k, R) != r) | (c != r))
        def _(k=k):
            hello((lax.rem(r + k, R), r, d))
    for k in range(C):
        @pl.when((lax.rem(c + k, C) != c) | (c != r))
        def _(k=k):
            hello((c, lax.rem(c + k, C), d))

    p[T * RB] = jnp.zeros((BS, LANES), jnp.bfloat16)
    n_hello = (R - 1) + (C * D - 1) + R + C
    pl.semaphore_wait(barrier, n_hello - 2 * jnp.where(r == c, 1, 0))

    left = lax.broadcasted_iota(jnp.int32, (BS, LANES), 1) < BS

    def placed(i, j):
        def pick(code):
            tile = p[code >> 1]
            moved = jnp.concatenate([tile[:, BS:], tile[:, :BS]], axis=1)
            return jnp.where(jnp.full((BS, LANES), code & 1) == 1, moved, tile)

        return jnp.where(left, pick(codes[i, 2 * j]), pick(codes[i, 2 * j + 1]))

    for t in range(T):
        load(t).wait()

    @pl.when(c == cs)
    def _():
        for q in range(C):
            def extract(j, _, q=q):
                panel[q, pl.ds(pl.multiple_of(j * BS, BS), BS), :] = placed(q * PB + j, window)
                return 0

            lax.fori_loop(0, PB, extract, 0)
            dst = x1.at[pl.ds(q * PR, PR)]

            @pl.when((q == r) & (r == c))
            def _(q=q, dst=dst):
                pltpu.make_async_copy(panel.at[q], dst, scat_recv).start()

            @pl.when((q != r) | (r != c))
            def _(q=q, dst=dst):
                remote(panel.at[q], dst, scat_send.at[q], scat_recv, (q, r, d)).start()

    def densify(i, _):
        rows = pl.ds(pl.multiple_of(i * BS, BS), BS)
        for j in range(T):
            dense[rows, j * LANES:(j + 1) * LANES] = placed(i, j)
        return 0

    lax.fori_loop(0, RB, densify, 0)

    mine = x1.at[pl.ds(pl.multiple_of(r * PR, PR), PR)]
    pltpu.make_async_copy(mine, mine, scat_recv).wait()

    def gather1(k):
        return remote(mine, mine, ag1_send.at[k], ag1_recv.at[k], (lax.rem(r + k, R), c, d))

    order = sorted(range(1, R), key=lambda k: -min(k, R - k))
    for k in order:
        gather1(k).start()
    def term(x, q, piece):
        at = pl.multiple_of(piece * PR, PR)
        return jnp.dot(
            dense[pl.ds(pl.multiple_of(q * PR, PR), PR), pl.ds(at, PR)], x[pl.ds(at, PR), :],
            preferred_element_type=jnp.float32)

    def first(x, piece):
        def one(q, _):
            part[q] = term(x, q, piece)
            return 0

        lax.fori_loop(0, C, one, 0)

    def more(x, piece):
        def one(q, _):
            part[q] += term(x, q, piece)
            return 0

        lax.fori_loop(0, C, one, 0)

    first(x1, r)
    near = order[::-1]
    for k in near:
        gather1(k).wait_recv()
        if k != near[-1]:
            more(x1, lax.rem(r + R - k, R))

    def reduce1(k):
        q = lax.rem(c + k, C)
        return remote(part.at[q], recv.at[c], rs_send.at[k], rs_recv.at[k], (r, q, d))

    for k in [*range(1, C), 0]:
        q = lax.rem(c + k, C)
        part[q] += term(x1, q, lax.rem(r + R - near[-1], R))
        if k:
            reduce1(k).start()
    total = part[c]
    for k in range(1, C):
        src = lax.rem(c + C - k, C)
        remote(part.at[0], recv.at[src], rs_send.at[k], rs_recv.at[k], (r, c, d)).wait_recv()
        total = total + recv[src]
    square[...] = total
    slot = pl.ds(pl.multiple_of(c * PR, PR), PR)
    rounded[...] = total.astype(jnp.bfloat16)

    def gather2(k):
        z = lax.rem(r + k, R)
        return remote(rounded, x2.at[slot], ag2_send.at[k], ag2_recv.at[c], (z, r, d))

    for k in order:
        gather2(k).start()

    @pl.when(r == c)
    def _():
        pltpu.make_async_copy(rounded, x2.at[slot], ag2_recv.at[c]).start()

    @pl.when(r != c)
    def _():
        gather2(0).start()

    def give(e):
        return remote(
            square.at[pl.ds(pl.multiple_of(lax.rem(d + e, D) * BS, BS), BS)], owned.at[d],
            sq_send.at[e], sq_recv.at[e], (r, c, lax.rem(d + e, D)))

    for e in range(1, D):
        give(e).start()
    for k in range(1, C):
        reduce1(k).wait_send()
    for q in range(C):
        piece = x2.at[pl.ds(q * PR, PR)]
        pltpu.make_async_copy(piece, piece, ag2_recv.at[q]).wait()
        if q == 0:
            first(x2, q)
        elif q < C - 1:
            more(x2, q)

    def blockrow(q, e):
        return part.at[q, pl.ds(pl.multiple_of(e * BS, BS), BS)]

    def cube(k, e):
        q, to = lax.rem(c + k, C), lax.rem(d + e, D)
        return remote(
            blockrow(q, to), cubes.at[c * D + d], cu_send.at[k * D + e], cu_recv, (r, q, to))

    for k in [*range(1, C), 0]:
        q = lax.rem(c + k, C)
        part[q] += term(x2, q, C - 1)
        for e in [2, 1, 3, 0]:
            if k or e:
                cube(k, e).start()
    pltpu.make_async_copy(blockrow(c, d), cubes.at[c * D + d], cu_recv).start()
    pltpu.make_async_copy(cubes, cubes, cu_recv).wait()
    own = square[pl.ds(pl.multiple_of(d * BS, BS), BS), :]
    for e in range(1, D):
        give(e).wait_recv()
    for e in range(D):
        sq = jnp.where(d == e, own, owned[e])
        total = cubes[e]
        for q in range(1, C):
            total = total + cubes[q * D + e]
        out[:, e * LANES:(e + 1) * LANES] = 3.0 * sq - 2.0 * total

    @pl.when(c == cs)
    def _():
        for q in range(C):
            @pl.when((q != r) | (r != c))
            def _(q=q):
                remote(panel.at[q], panel.at[q], scat_send.at[q], scat_recv, (q, r, d)).wait_send()

    for k in order:
        gather1(k).wait_send()
        gather2(k).wait_send()

    @pl.when(r != c)
    def _():
        gather2(0).wait_send()

    for e in range(1, D):
        give(e).wait_send()
    for k in range(C):
        for e in range(D):
            if k or e:
                cube(k, e).wait_send()


def body(p_blocks, p_cols, out_mask):
    R, C, D = lax.axis_size("row"), lax.axis_size("col"), lax.axis_size("depth")
    RB, BS, K = p_blocks.shape
    WB = out_mask.shape[1]
    PR = RB // C * BS
    bf, f32 = jnp.bfloat16, jnp.float32
    dma = pltpu.SemaphoreType.DMA
    T = K // LANES
    places = jnp.arange(RB, dtype=jnp.int32)
    wanted = lax.axis_index("col") * RB + places
    slot = jnp.max(
        jnp.where(p_cols[:, :, None] == wanted, places[None, :, None], -1), axis=1)
    tile = (slot // 2) * RB + places[:, None]
    codes = jnp.where(slot < 0, 2 * T * RB, 2 * tile + (slot % 2 != places % 2))
    rows = pl.pallas_call(
        functools.partial(kernel, R, C, D, RB, BS, WB),
        out_shape=jax.ShapeDtypeStruct((BS, WB * BS), f32),
        in_specs=[pl.BlockSpec(memory_space=pl.ANY), pl.BlockSpec(memory_space=pltpu.SMEM)],
        out_specs=pl.BlockSpec(memory_space=pltpu.VMEM),
        scratch_shapes=[
            pltpu.VMEM((T * RB + 1, BS, LANES), bf),
            pltpu.VMEM((K, K), bf),
            pltpu.VMEM((C, PR, LANES), bf),
            pltpu.VMEM((K, LANES), bf),
            pltpu.VMEM((K, LANES), bf),
            pltpu.VMEM((C, PR, LANES), f32),
            pltpu.VMEM((C, PR, LANES), f32),
            pltpu.VMEM((PR, LANES), f32),
            pltpu.VMEM((PR, LANES), bf),
            pltpu.VMEM((C * D, BS, LANES), f32),
            pltpu.VMEM((D, BS, LANES), f32),
            dma((T,)), dma((C,)), dma, dma((R,)), dma((R,)), dma((C,)), dma((C,)),
            dma((R,)), dma((C,)), dma((D,)), dma((D,)), dma((C * D,)), dma,
        ],
        compiler_params=pltpu.CompilerParams(
            collective_id=0, has_side_effects=True, vmem_limit_bytes=48 << 20),
    )(p_blocks, codes)
    shaped = rows.reshape(1, BS, WB, BS) * out_mask.astype(f32)[:, None, :, None]
    return shaped.reshape(1, BS, WB * BS)


def solution(mesh):
    in_specs = (P("row", None, "col"), P("row", "col"), P(("row", "col", "depth"), None))
    out_specs = P(("row", "col", "depth"), None, None)
    return jax.shard_map(body, mesh=mesh, in_specs=in_specs, out_specs=out_specs, check_vma=False)
```

time: 703 us -> 93.7 us (0.13)
  the two profiles are of different devices: /device:TPU:1 before, /device:TPU:27 now
where the time goes in v1:
time: 93.7 us; the launch traced here: 93.5 us
  Pallas kernels  91.7 us (98%)
  other arithmetic  1.67 us (2%)
    pallas_call x1, Pallas kernels, body(): pl.pallas_call(functools.partial(kernel, R, C, D, RB, BS, WB), out_shape=...  91.7 us

profile of v1, /device:TPU:27, one launch (start us, length us, event | category | flops | bytes accessed | tf_op | source)
XLA Modules:
  0.0 93.5 jit_solution(6692899749316991954)
XLA Ops:
  0.0 0.0 copy-start
  0.0 1.0 %select_reduce_fusion = s32[32,32]{1,0:T(8,128)S(1)} fusion(s32[32]{0:T(128)S(1)} %iota_add_fusion, s32[32,32]{1,0:T(8,128)} %param.4), kind=kLoop, calls=%fused_computation | loop fusion | flops 97280 | bytes 8320 | tf_op jit(solution)/shard_map/reduce_max | solution.py:250
  1.0 91.7 %shard_map.37 = f32[64,512]{1,0:T(8,128)S(1)} custom-call(bf16[32,64,2048]{2,1,0:T(8,128)(2,1)} %p_hbm.1, s32[32,32]{1,0:T(8,128)S(1)} %fusion.4.codes), custom_call_target="tpu_custom_call" | custom-call | tf_op jit(solution)/shard_map/pallas_call | solution.py:254
  92.7 0.0 copy-done
  92.7 0.1 mul.38
  92.8 0.1 mul.39
  92.9 0.7 multiply_bitcast_fusion
  (4 shorter events, 0.0 us)
Async XLA Ops:
  0.0 92.7 %copy-start = (s32[1,8]{1,0:T(1,128)S(1)}, s32[1,8]{1,0:T(1,128)}, u32[]{:S(2)}) copy-start(s32[1,8]{1,0:T(1,128)} %param.5) | copy-start | bytes 100

commit v2 on v1

v2 whole, which is shorter than its diff:
```python
import functools

import jax
import jax.numpy as jnp
from jax import lax
from jax.experimental import pallas as pl
from jax.experimental.pallas import tpu as pltpu
from jax.sharding import PartitionSpec as P

MESH = pl.DeviceIdType.MESH
LANES = 128


def kernel(
    R, C, D, RB, BS,
    p_hbm, codes, out,
    p, dense, panel, x1, x2, part, core1, core2, recv, square, rounded, cubes, owned,
    load_sem, scat_send, in1, ag1_send, ag1_recv, core1_send, core1_recv, rs_send, rs_recv,
    turn_send, in2, ag2_send, ag2_recv, sq_send, sq_recv, core2_send, core2_recv,
    cu_send, cu_recv,
):
    r, c, d = lax.axis_index("row"), lax.axis_index("col"), lax.axis_index("depth")
    PB = RB // C
    PR = PB * BS
    K = RB * BS
    T = K // LANES
    H, Y, half, each = R // 2, C // 2, D // 2, C // D
    y, core = c // 2, lax.rem(c, 2)
    sibling = (r, c + 1 - 2 * core, d)
    side = c // Y
    source = lax.rem(c, Y) == 0

    def remote(src, dst, ss, rs, did):
        return pltpu.make_async_remote_copy(
            src_ref=src, dst_ref=dst, send_sem=ss, recv_sem=rs,
            device_id=did, device_id_type=MESH)

    def is_self(did):
        return (did[0] == r) & (did[1] == c) & (did[2] == d)

    def piece_of(x, q):
        return x.at[pl.ds(pl.multiple_of(q * PR, PR), PR)]

    def load(t):
        return pltpu.make_async_copy(
            p_hbm.at[:, :, pl.ds(t * LANES, LANES)], p.at[pl.ds(t * RB, RB)], load_sem.at[t])

    for t in range(T):
        load(t).start()

    scatter = []
    for u in range(each):
        for w in range(half):
            for v in range(2):
                q = d * each + u
                scatter.append((u, w, v, q, (lax.rem(q + v * H, R), r, side * half + w)))
    hops = [k for n in range(H // 2, 0, -1) for k in (n, R - n)]
    hops = list(dict.fromkeys(hops))
    turned = [(lax.rem(c + v * H, R), r, d) for v in range(2)]

    barrier = pltpu.get_barrier_semaphore()

    def hello(did):
        pl.semaphore_signal(barrier, inc=1, device_id=did, device_id_type=MESH)

    def hello_other(did):
        @pl.when(jnp.logical_not(is_self(did)))
        def _():
            hello(did)

    for v in range(2):
        q = lax.rem(r + v * H, R)
        hello_other((c, (d // half) * Y, q // each))
        hello_other((c, q, d))
    for k in hops:
        hello((lax.rem(r + k, R), c, d))
    hello(sibling)
    for k in range(Y):
        for e in range(D):
            if k or e:
                hello((r, 2 * lax.rem(y + k, Y) + core, lax.rem(d + e, D)))

    def others(dids):
        return sum(jnp.where(is_self(did), 0, 1) for did in dids)

    p[T * RB] = jnp.zeros((BS, LANES), jnp.bfloat16)
    panels = others([s[-1] for s in scatter])
    pl.semaphore_wait(
        barrier, len(hops) + Y * D + others(turned) + jnp.where(source, panels, 0))

    left = lax.broadcasted_iota(jnp.int32, (BS, LANES), 1) < BS

    def placed(i, j):
        def pick(code):
            tile = p[code >> 1]
            moved = jnp.concatenate([tile[:, BS:], tile[:, :BS]], axis=1)
            return jnp.where(jnp.full((BS, LANES), code & 1) == 1, moved, tile)

        return jnp.where(left, pick(codes[i, 2 * j]), pick(codes[i, 2 * j + 1]))

    for t in range(T):
        load(t).wait()

    def panel_copy(u, w, v, q, did):
        return remote(panel.at[u, w], piece_of(x1, q), scat_send.at[u, w, v], in1.at[v], did)

    @pl.when(source)
    def _():
        for u in range(each):
            def extract(j, _, u=u):
                rows = pl.ds(pl.multiple_of(j * BS, BS), BS)
                for w in range(half):
                    panel[u, w, rows, :] = placed((d * each + u) * PB + j, w)
                return 0

            lax.fori_loop(0, PB, extract, 0)
            for s in scatter:
                if s[0] == u:
                    @pl.when(is_self(s[-1]))
                    def _(s=s):
                        pltpu.make_async_copy(
                            panel.at[s[0], s[1]], piece_of(x1, s[3]), in1.at[s[2]]).start()

                    @pl.when(jnp.logical_not(is_self(s[-1])))
                    def _(s=s):
                        panel_copy(*s).start()

    def densify(i, _):
        rows = pl.ds(pl.multiple_of(i * BS, BS), BS)
        for j in range(T):
            dense[rows, j * LANES:(j + 1) * LANES] = placed(i, j)
        return 0

    lax.fori_loop(0, RB, densify, 0)

    def spread(x, arrived, sends, recvs):
        def copy(v, k):
            at = piece_of(x, lax.rem(r + v * H, R))
            return remote(at, at, sends.at[v, k], recvs.at[v, k], (lax.rem(r + k, R), c, d))

        moves = [(v, k) for v in range(2) for k in hops if v == 0 or 2 * min(k, R - k) < H]
        for v in range(2):
            at = piece_of(x, lax.rem(r + v * H, R))
            pltpu.make_async_copy(at, at, arrived.at[v]).wait()
            for move in moves:
                if move[0] == v:
                    copy(*move).start()
        for move in moves:
            copy(*move).wait_recv()
        return [copy(*move) for move in moves]

    def product(x, q):
        rows = pl.ds(pl.multiple_of(q * PR, PR), PR)
        part[q] = jnp.dot(dense[rows, :], x[...], preferred_element_type=jnp.float32)

    far = sorted(range(1, Y), key=lambda k: -min(k, Y - k)) + [0]

    def to_sibling(x, k, buffer, sends, recvs):
        m = lax.rem(y + k, Y)
        q = 2 * m + 1 - core
        return q, remote(part.at[q], buffer.at[k], sends.at[k], recvs.at[k], sibling)

    def with_sibling(x, buffer, sends, recvs, then):
        for k in far:
            q, copy = to_sibling(x, k, buffer, sends, recvs)
            product(x, q)
            copy.start()
        for k in far:
            q = 2 * lax.rem(y + k, Y) + core
            product(x, q)
            to_sibling(x, k, buffer, sends, recvs)[1].wait_recv()
            part[q] += buffer[k]
            then(k, q)

    sent1 = spread(x1, in1, ag1_send, ag1_recv)

    def reduce1(k):
        q = 2 * lax.rem(y + k, Y) + core
        return remote(part.at[q], recv.at[k], rs_send.at[k], rs_recv.at[k], (r, q, d))

    def send1(k, q):
        if k:
            reduce1(k).start()

    with_sibling(x1, core1, core1_send, core1_recv, send1)
    total = part[c]
    for k in range(1, Y):
        reduce1(k).wait_recv()
        total = total + recv[k]
    square[...] = total
    rounded[...] = total.astype(jnp.bfloat16)

    def turn(v):
        return remote(rounded, piece_of(x2, c), turn_send.at[v], in2.at[v], turned[v])

    for v in range(2):
        @pl.when(is_self(turned[v]))
        def _(v=v):
            pltpu.make_async_copy(rounded, piece_of(x2, c), in2.at[v]).start()

        @pl.when(jnp.logical_not(is_self(turned[v])))
        def _(v=v):
            turn(v).start()

    def give(e):
        to = lax.rem(d + e, D)
        return remote(
            square.at[pl.ds(pl.multiple_of(to * BS, BS), BS)], owned.at[d],
            sq_send.at[e], sq_recv.at[e], (r, c, to))

    sent2 = spread(x2, in2, ag2_send, ag2_recv)
    for e in range(1, D):
        give(e).start()
    for k in range(Y):
        to_sibling(x1, k, core1, core1_send, core1_recv)[1].wait_send()
        if k:
            reduce1(k).wait_send()

    def cube(k, e):
        q, to = 2 * lax.rem(y + k, Y) + core, lax.rem(d + e, D)
        return remote(
            part.at[q, pl.ds(pl.multiple_of(to * BS, BS), BS)], cubes.at[y * D + d],
            cu_send.at[k * D + e], cu_recv, (r, q, to))

    def send2(k, q):
        for e in sorted(range(D), key=lambda e: -min(e, D - e)):
            if k or e:
                cube(k, e).start()
            else:
                pltpu.make_async_copy(
                    part.at[q, pl.ds(pl.multiple_of(d * BS, BS), BS)], cubes.at[y * D + d],
                    cu_recv).start()

    with_sibling(x2, core2, core2_send, core2_recv, send2)
    for e in range(1, D):
        give(e).wait_recv()
    pltpu.make_async_copy(cubes, cubes, cu_recv).wait()
    own = square[pl.ds(pl.multiple_of(d * BS, BS), BS), :]
    for e in range(D):
        total = cubes[e]
        for m in range(1, Y):
            total = total + cubes[m * D + e]
        out[:, e * LANES:(e + 1) * LANES] = 3.0 * jnp.where(d == e, own, owned[e]) - 2.0 * total

    @pl.when(source)
    def _():
        for s in scatter:
            @pl.when(jnp.logical_not(is_self(s[-1])))
            def _(s=s):
                panel_copy(*s).wait_send()

    for copy in sent1 + sent2:
        copy.wait_send()
    for v in range(2):
        @pl.when(jnp.logical_not(is_self(turned[v])))
        def _(v=v):
            turn(v).wait_send()

    for e in range(1, D):
        give(e).wait_send()
    for k in range(Y):
        to_sibling(x2, k, core2, core2_send, core2_recv)[1].wait_send()
        for e in range(D):
            if k or e:
                cube(k, e).wait_send()


def body(p_blocks, p_cols, out_mask):
    R, C, D = lax.axis_size("row"), lax.axis_size("col"), lax.axis_size("depth")
    RB, BS, K = p_blocks.shape
    WB = out_mask.shape[1]
    PR = RB // C * BS
    T, Y = K // LANES, C // 2
    bf, f32 = jnp.bfloat16, jnp.float32
    dma = pltpu.SemaphoreType.DMA
    places = jnp.arange(RB, dtype=jnp.int32)
    wanted = lax.axis_index("col") * RB + places
    slot = jnp.max(
        jnp.where(p_cols[:, :, None] == wanted, places[None, :, None], -1), axis=1)
    tile = (slot // 2) * RB + places[:, None]
    codes = jnp.where(slot < 0, 2 * T * RB, 2 * tile + (slot % 2 != places % 2))
    rows = pl.pallas_call(
        functools.partial(kernel, R, C, D, RB, BS),
        out_shape=jax.ShapeDtypeStruct((BS, WB * BS), f32),
        in_specs=[pl.BlockSpec(memory_space=pl.ANY), pl.BlockSpec(memory_space=pltpu.SMEM)],
        out_specs=pl.BlockSpec(memory_space=pltpu.VMEM),
        scratch_shapes=[
            pltpu.VMEM((T * RB + 1, BS, LANES), bf),
            pltpu.VMEM((K, K), bf),
            pltpu.VMEM((C // D, D // 2, PR, LANES), bf),
            pltpu.VMEM((K, LANES), bf),
            pltpu.VMEM((K, LANES), bf),
            pltpu.VMEM((C, PR, LANES), f32),
            pltpu.VMEM((Y, PR, LANES), f32),
            pltpu.VMEM((Y, PR, LANES), f32),
            pltpu.VMEM((Y, PR, LANES), f32),
            pltpu.VMEM((PR, LANES), f32),
            pltpu.VMEM((PR, LANES), bf),
            pltpu.VMEM((Y * D, BS, LANES), f32),
            pltpu.VMEM((D, BS, LANES), f32),
            dma((T,)), dma((C // D, D // 2, 2)), dma((2,)), dma((2, R)), dma((2, R)),
            dma((Y,)), dma((Y,)), dma((Y,)), dma((Y,)),
            dma((2,)), dma((2,)), dma((2, R)), dma((2, R)), dma((D,)), dma((D,)),
            dma((Y,)), dma((Y,)), dma((Y * D,)), dma,
        ],
        compiler_params=pltpu.CompilerParams(
            collective_id=0, has_side_effects=True, vmem_limit_bytes=48 << 20),
    )(p_blocks, codes)
    shaped = rows.reshape(1, BS, WB, BS) * out_mask.astype(f32)[:, None, :, None]
    return shaped.reshape(1, BS, WB * BS)


def solution(mesh):
    in_specs = (P("row", None, "col"), P("row", "col"), P(("row", "col", "depth"), None))
    out_specs = P(("row", "col", "depth"), None, None)
    return jax.shard_map(body, mesh=mesh, in_specs=in_specs, out_specs=out_specs, check_vma=False)
```

time: 93.7 us -> 66.3 us (0.71)
  the two profiles are of different devices: /device:TPU:27 before, /device:TPU:1 now
where the time goes in v2:
time: 66.3 us; the launch traced here: 65.9 us
  Pallas kernels  64 us (97%)
  other arithmetic  1.67 us (3%)
    pallas_call x1, Pallas kernels, body(): pl.pallas_call(functools.partial(kernel, R, C, D, RB, BS), out_shape=jax....  64 us

profile of v2, /device:TPU:1, one launch (start us, length us, event | category | flops | bytes accessed | tf_op | source)
XLA Modules:
  0.0 65.9 jit_solution(7720606963409371322)
XLA Ops:
  0.0 0.0 copy-start
  0.0 1.0 %select_reduce_fusion = s32[32,32]{1,0:T(8,128)S(1)} fusion(s32[32]{0:T(128)S(1)} %iota_add_fusion, s32[32,32]{1,0:T(8,128)} %param.4), kind=kLoop, calls=%fused_computation | loop fusion | flops 97280 | bytes 8320 | tf_op jit(solution)/shard_map/reduce_max | solution.py:278
  1.0 64.0 %shard_map.37 = f32[64,512]{1,0:T(8,128)S(1)} custom-call(bf16[32,64,2048]{2,1,0:T(8,128)(2,1)} %p_hbm.1, s32[32,32]{1,0:T(8,128)S(1)} %fusion.4.codes), custom_call_target="tpu_custom_call" | custom-call | tf_op jit(solution)/shard_map/pallas_call | solution.py:282
  65.0 0.0 copy-done
  65.1 0.1 mul.38
  65.1 0.1 mul.39
  65.2 0.7 %multiply_bitcast_fusion = f32[1,64,512]{2,1,0:T(8,128)} fusion(f32[64,512]{1,0:T(8,128)S(1)} %shard_map.37, f32[512]{0:T(512)S(1)} %mul.39), kind=kLoop, calls=%fused_computation.1 | loop fusion | flops 32768 | bytes 264192 | tf_op jit(solution)/shard_map/mul | solution.py:309
  (4 shorter events, 0.0 us)
Async XLA Ops:
  0.0 65.0 %copy-start = (s32[1,8]{1,0:T(1,128)S(1)}, s32[1,8]{1,0:T(1,128)}, u32[]{:S(2)}) copy-start(s32[1,8]{1,0:T(1,128)} %param.5) | copy-start | bytes 100

commit v3 on v2

--- a/solution.py
+++ b/solution.py
@@ -13,9 +13,9 @@
 
 def kernel(
     R, C, D, RB, BS,
-    p_hbm, codes, out,
-    p, dense, panel, x1, x2, part, core1, core2, recv, square, rounded, cubes, owned,
-    load_sem, scat_send, in1, ag1_send, ag1_recv, core1_send, core1_recv, rs_send, rs_recv,
+    p_hbm, cols, out,
+    table, codes, p, dense, panel, x1, x2, part, core1, core2, sent, recv, square, rounded, shares, cubes, owned,
+    table_sem, load_sem, scat_send, in1, ag1_send, ag1_recv, core1_send, core1_recv, rs_send, rs_recv,
     turn_send, in2, ag2_send, ag2_recv, sq_send, sq_recv, core2_send, core2_recv,
     cu_send, cu_recv,
 ):
@@ -24,7 +24,7 @@
     PR = PB * BS
     K = RB * BS
     T = K // LANES
-    H, Y, half, each = R // 2, C // 2, D // 2, C // D
+    H, Y, half = R // 2, C // 2, D // 2
     y, core = c // 2, lax.rem(c, 2)
     sibling = (r, c + 1 - 2 * core, d)
     side = c // Y
@@ -41,19 +41,17 @@
     def piece_of(x, q):
         return x.at[pl.ds(pl.multiple_of(q * PR, PR), PR)]
 
+    def block_of(x, i):
+        return x.at[pl.ds(pl.multiple_of(i * BS, BS), BS)]
+
     def load(t):
         return pltpu.make_async_copy(
             p_hbm.at[:, :, pl.ds(t * LANES, LANES)], p.at[pl.ds(t * RB, RB)], load_sem.at[t])
 
-    for t in range(T):
-        load(t).start()
-
-    scatter = []
-    for u in range(each):
-        for w in range(half):
-            for v in range(2):
-                q = d * each + u
-                scatter.append((u, w, v, q, (lax.rem(q + v * H, R), r, side * half + w)))
+    scatter = [
+        (q, w, v, ((q + v * H) % R, r, side * half + w))
+        for q in range(C) for v in range(2) for w in range(half)]
+    receivers = [(z, r, side * half + w) for z in range(R) for w in range(half)]
     hops = [k for n in range(H // 2, 0, -1) for k in (n, R - n)]
     hops = list(dict.fromkeys(hops))
     turned = [(lax.rem(c + v * H, R), r, d) for v in range(2)]
@@ -68,10 +66,10 @@
         def _():
             hello(did)
 
+    for e in range(D):
+        hello_other((c, (d // half) * Y, lax.rem(d + e, D)))
     for v in range(2):
-        q = lax.rem(r + v * H, R)
-        hello_other((c, (d // half) * Y, q // each))
-        hello_other((c, q, d))
+        hello_other((c, lax.rem(r + v * H, R), d))
     for k in hops:
         hello((lax.rem(r + k, R), c, d))
     hello(sibling)
@@ -83,8 +81,22 @@
     def others(dids):
         return sum(jnp.where(is_self(did), 0, 1) for did in dids)
 
+    for t in range(T):
+        load(t).start()
+
+    row = lax.broadcasted_iota(jnp.int32, (RB, LANES), 0)
+    place = lax.broadcasted_iota(jnp.int32, (RB, LANES), 1)
+    local = cols[...] - c * RB
+    code = jnp.full((RB, LANES), 2 * T * RB, jnp.int32)
+    for u in range(RB):
+        at = 2 * ((u // 2) * RB + row) + ((place & 1) ^ (u & 1))
+        code = jnp.where(local[:, u:u + 1] == place, at, code)
+    table[...] = code
+    fill = pltpu.make_async_copy(table, codes, table_sem)
+    fill.start()
     p[T * RB] = jnp.zeros((BS, LANES), jnp.bfloat16)
-    panels = others([s[-1] for s in scatter])
+    fill.wait()
+    panels = others(receivers)
     pl.semaphore_wait(
         barrier, len(hops) + Y * D + others(turned) + jnp.where(source, panels, 0))
 
@@ -101,29 +113,27 @@
     for t in range(T):
         load(t).wait()
 
-    def panel_copy(u, w, v, q, did):
-        return remote(panel.at[u, w], piece_of(x1, q), scat_send.at[u, w, v], in1.at[v], did)
+    def panel_copy(q, w, v, did):
+        return remote(
+            panel.at[q, w], block_of(x1, q * PB + d), scat_send.at[q, w, v], in1.at[v], did)
 
     @pl.when(source)
     def _():
-        for u in range(each):
-            def extract(j, _, u=u):
-                rows = pl.ds(pl.multiple_of(j * BS, BS), BS)
-                for w in range(half):
-                    panel[u, w, rows, :] = placed((d * each + u) * PB + j, w)
-                return 0
-
-            lax.fori_loop(0, PB, extract, 0)
-            for s in scatter:
-                if s[0] == u:
-                    @pl.when(is_self(s[-1]))
-                    def _(s=s):
-                        pltpu.make_async_copy(
-                            panel.at[s[0], s[1]], piece_of(x1, s[3]), in1.at[s[2]]).start()
-
-                    @pl.when(jnp.logical_not(is_self(s[-1])))
-                    def _(s=s):
-                        panel_copy(*s).start()
+        def extract(q, _):
+            for w in range(half):
+                panel[q, w] = placed(q * PB + d, w)
+            return 0
+
+        lax.fori_loop(0, C, extract, 0)
+        for s in scatter:
+            @pl.when(is_self(s[-1]))
+            def _(s=s):
+                pltpu.make_async_copy(
+                    panel.at[s[0], s[1]], block_of(x1, s[0] * PB + d), in1.at[s[2]]).start()
+
+            @pl.when(jnp.logical_not(is_self(s[-1])))
+            def _(s=s):
+                panel_copy(*s).start()
 
     def densify(i, _):
         rows = pl.ds(pl.multiple_of(i * BS, BS), BS)
@@ -153,6 +163,20 @@
         rows = pl.ds(pl.multiple_of(q * PR, PR), PR)
         part[q] = jnp.dot(dense[rows, :], x[...], preferred_element_type=jnp.float32)
 
+    def coded(value, ref):
+        n = value.shape[0]
+        top = jnp.maximum(jnp.max(jnp.abs(value), axis=0, keepdims=True), 1e-30)
+        level = jnp.ceil(jnp.log2(top) * 16.0) + 1.0
+        scaled = jnp.round(value * (jnp.exp2(level * -0.0625) * 32000.0))
+        ref[0:n, :] = scaled.astype(jnp.int32).astype(jnp.int16)
+        ref[n:n + 16, :] = jnp.broadcast_to(
+            level, (16, LANES)).astype(jnp.int32).astype(jnp.int16)
+
+    def decoded(ref, n):
+        level = ref[n:n + 16, :].astype(jnp.int32).astype(jnp.float32)[0:1, :]
+        scale = jnp.exp2(level * 0.0625) * (1.0 / 32000.0)
+        return ref[0:n, :].astype(jnp.int32).astype(jnp.float32) * scale
+
     far = sorted(range(1, Y), key=lambda k: -min(k, Y - k)) + [0]
 
     def to_sibling(x, k, buffer, sends, recvs):
@@ -169,24 +193,26 @@
             q = 2 * lax.rem(y + k, Y) + core
             product(x, q)
             to_sibling(x, k, buffer, sends, recvs)[1].wait_recv()
-            part[q] += buffer[k]
-            then(k, q)
+            then(k, q, part[q] + buffer[k])
 
     sent1 = spread(x1, in1, ag1_send, ag1_recv)
 
     def reduce1(k):
         q = 2 * lax.rem(y + k, Y) + core
-        return remote(part.at[q], recv.at[k], rs_send.at[k], rs_recv.at[k], (r, q, d))
-
-    def send1(k, q):
+        return remote(sent.at[k], recv.at[k], rs_send.at[k], rs_recv.at[k], (r, q, d))
+
+    def send1(k, q, value):
         if k:
+            coded(value, sent.at[k])
             reduce1(k).start()
+        else:
+            square[...] = value
 
     with_sibling(x1, core1, core1_send, core1_recv, send1)
-    total = part[c]
+    total = square[...]
     for k in range(1, Y):
         reduce1(k).wait_recv()
-        total = total + recv[k]
+        total = total + decoded(recv.at[k], PR)
     square[...] = total
     rounded[...] = total.astype(jnp.bfloat16)
 
@@ -219,17 +245,18 @@
     def cube(k, e):
         q, to = 2 * lax.rem(y + k, Y) + core, lax.rem(d + e, D)
         return remote(
-            part.at[q, pl.ds(pl.multiple_of(to * BS, BS), BS)], cubes.at[y * D + d],
+            shares.at[k * D + e], cubes.at[y * D + d],
             cu_send.at[k * D + e], cu_recv, (r, q, to))
 
-    def send2(k, q):
+    def send2(k, q, value):
+        part[q] = value
         for e in sorted(range(D), key=lambda e: -min(e, D - e)):
+            to = pl.ds(pl.multiple_of(lax.rem(d + e, D) * BS, BS), BS)
+            coded(part[q, to, :], shares.at[k * D + e])
             if k or e:
                 cube(k, e).start()
             else:
-                pltpu.make_async_copy(
-                    part.at[q, pl.ds(pl.multiple_of(d * BS, BS), BS)], cubes.at[y * D + d],
-                    cu_recv).start()
+                pltpu.make_async_copy(shares.at[0], cubes.at[y * D + d], cu_recv).start()
 
     with_sibling(x2, core2, core2_send, core2_recv, send2)
     for e in range(1, D):
@@ -237,9 +264,9 @@
     pltpu.make_async_copy(cubes, cubes, cu_recv).wait()
     own = square[pl.ds(pl.multiple_of(d * BS, BS), BS), :]
     for e in range(D):
-        total = cubes[e]
+        total = decoded(cubes.at[e], BS)
         for m in range(1, Y):
-            total = total + cubes[m * D + e]
+            total = total + decoded(cubes.at[m * D + e], BS)
         out[:, e * LANES:(e + 1) * LANES] = 3.0 * jnp.where(d == e, own, owned[e]) - 2.0 * total
 
     @pl.when(source)
@@ -273,39 +300,37 @@
     T, Y = K // LANES, C // 2
     bf, f32 = jnp.bfloat16, jnp.float32
     dma = pltpu.SemaphoreType.DMA
-    places = jnp.arange(RB, dtype=jnp.int32)
-    wanted = lax.axis_index("col") * RB + places
-    slot = jnp.max(
-        jnp.where(p_cols[:, :, None] == wanted, places[None, :, None], -1), axis=1)
-    tile = (slot // 2) * RB + places[:, None]
-    codes = jnp.where(slot < 0, 2 * T * RB, 2 * tile + (slot % 2 != places % 2))
     rows = pl.pallas_call(
         functools.partial(kernel, R, C, D, RB, BS),
         out_shape=jax.ShapeDtypeStruct((BS, WB * BS), f32),
-        in_specs=[pl.BlockSpec(memory_space=pl.ANY), pl.BlockSpec(memory_space=pltpu.SMEM)],
+        in_specs=[pl.BlockSpec(memory_space=pl.ANY), pl.BlockSpec(memory_space=pltpu.VMEM)],
         out_specs=pl.BlockSpec(memory_space=pltpu.VMEM),
         scratch_shapes=[
+            pltpu.VMEM((RB, LANES), jnp.int32),
+            pltpu.SMEM((RB, LANES), jnp.int32),
             pltpu.VMEM((T * RB + 1, BS, LANES), bf),
             pltpu.VMEM((K, K), bf),
-            pltpu.VMEM((C // D, D // 2, PR, LANES), bf),
+            pltpu.VMEM((C, D // 2, BS, LANES), bf),
             pltpu.VMEM((K, LANES), bf),
             pltpu.VMEM((K, LANES), bf),
             pltpu.VMEM((C, PR, LANES), f32),
             pltpu.VMEM((Y, PR, LANES), f32),
             pltpu.VMEM((Y, PR, LANES), f32),
-            pltpu.VMEM((Y, PR, LANES), f32),
+            pltpu.VMEM((Y, PR + 16, LANES), jnp.int16),
+            pltpu.VMEM((Y, PR + 16, LANES), jnp.int16),
             pltpu.VMEM((PR, LANES), f32),
             pltpu.VMEM((PR, LANES), bf),
-            pltpu.VMEM((Y * D, BS, LANES), f32),
+            pltpu.VMEM((Y * D, BS + 16, LANES), jnp.int16),
+            pltpu.VMEM((Y * D, BS + 16, LANES), jnp.int16),
             pltpu.VMEM((D, BS, LANES), f32),
-            dma((T,)), dma((C // D, D // 2, 2)), dma((2,)), dma((2, R)), dma((2, R)),
+            dma, dma((T,)), dma((C, D // 2, 2)), dma((2,)), dma((2, R)), dma((2, R)),
             dma((Y,)), dma((Y,)), dma((Y,)), dma((Y,)),
             dma((2,)), dma((2,)), dma((2, R)), dma((2, R)), dma((D,)), dma((D,)),
             dma((Y,)), dma((Y,)), dma((Y * D,)), dma,
         ],
         compiler_params=pltpu.CompilerParams(
             collective_id=0, has_side_effects=True, vmem_limit_bytes=48 << 20),
-    )(p_blocks, codes)
+    )(p_blocks, p_cols)
     shaped = rows.reshape(1, BS, WB, BS) * out_mask.astype(f32)[:, None, :, None]
     return shaped.reshape(1, BS, WB * BS)
 

time: 66.3 us -> 61.4 us (0.926)
  Pallas kernels: 64 us -> 59.1 us
  local copies, waits for them, and re-layouts: 0.15 us -> 0.87 us
    pallas_call x1, Pallas kernels: 64 us -> 59.1 us  [body(): pl.pallas_call(functools.partial(kernel, R, C, D, RB, BS), out_shape=jax....]
    reduce_max x1 -> x0, other arithmetic: 0.96 us -> none  [body(): jnp.max(jnp.where(p_cols[:, :, None] == wanted, places[None, :, None], -1...]
    unnamed x2, local copies, waits for them, and re-layouts: 0.01 us -> 0.72 us
where the time goes in v3:
time: 61.4 us; the launch traced here: 61.3 us
  Pallas kernels  59.1 us (96%)
  other arithmetic  1.33 us (2%)
  local copies, waits for them, and re-layouts  0.87 us (1%)
    pallas_call x1, Pallas kernels, body(): pl.pallas_call(functools.partial(kernel, R, C, D, RB, BS), out_shape=jax....  59.1 us
    mul x2, other arithmetic, body(): rows.reshape(1, BS, WB, BS) * out_mask.astype(f32)[:, None, :, None]  1.33 us

profile of v3, /device:TPU:1, one launch (start us, length us, event | category | flops | bytes accessed | tf_op | source)
XLA Modules:
  0.0 61.3 jit_solution(7753068930580783649)
XLA Ops:
  0.0 0.7 %convert_bitcast_fusion = f32[8]{0:T(128)S(1)} fusion(s32[1,8]{1,0:T(1,128)} %param.5), kind=kLoop, calls=%fused_computation.1 | loop fusion | flops 8 | bytes 64 | tf_op jit(solution)/shard_map/mul | solution.py:334
  0.7 0.1 mul.21
  0.7 0.1 mul.22
  0.8 0.0 copy-start
  0.8 0.7 %copy-done = s32[32,32]{1,0:T(8,128)S(1)} copy-done((s32[32,32]{1,0:T(8,128)S(1)}, s32[32,32]{1,0:T(8,128)}, u32[]{:S(2)}) %copy-start) | copy-done | bytes 4120
  1.5 59.1 %shard_map.37 = f32[64,512]{1,0:T(8,128)S(1)} custom-call(bf16[32,64,2048]{2,1,0:T(8,128)(2,1)} %p_hbm.1, s32[32,32]{1,0:T(8,128)S(1)} %copy-done), custom_call_target="tpu_custom_call" | custom-call | tf_op jit(solution)/shard_map/pallas_call | solution.py:303
  60.6 0.7 %multiply_bitcast_fusion = f32[1,64,512]{2,1,0:T(8,128)} fusion(f32[64,512]{1,0:T(8,128)S(1)} %shard_map.37, f32[512]{0:T(512)S(1)} %mul.22), kind=kLoop, calls=%fused_computation | loop fusion | flops 32768 | bytes 264192 | tf_op jit(solution)/shard_map/mul | solution.py:334
Async XLA Ops:
  0.8 0.7 %copy-start = (s32[32,32]{1,0:T(8,128)S(1)}, s32[32,32]{1,0:T(8,128)}, u32[]{:S(2)}) copy-start(s32[32,32]{1,0:T(8,128)} %cols.1) | copy-start | bytes 12292

commit v4 on v3

--- a/solution.py
+++ b/solution.py
@@ -38,11 +38,17 @@
     def is_self(did):
         return (did[0] == r) & (did[1] == c) & (did[2] == d)
 
-    def piece_of(x, q):
-        return x.at[pl.ds(pl.multiple_of(q * PR, PR), PR)]
-
-    def block_of(x, i):
-        return x.at[pl.ds(pl.multiple_of(i * BS, BS), BS)]
+    own = list(dict.fromkeys([0, H]))
+    far = [k for k in range(R) if k not in own]
+    near = [k for k in range(R) if k not in own + far]
+    spot = {k: n for n, k in enumerate(own + near + far)}
+    cut1, cut2 = len(own) * PR, len(own + near) * PR
+
+    def piece_at(x, k):
+        return x.at[spot[k % R] * PR:(spot[k % R] + 1) * PR]
+
+    def block_at(x, k, j):
+        return x.at[pl.ds(pl.multiple_of(spot[k] * PR + j * BS, BS), BS)]
 
     def load(t):
         return pltpu.make_async_copy(
@@ -50,7 +56,7 @@
 
     scatter = [
         (q, w, v, ((q + v * H) % R, r, side * half + w))
-        for q in range(C) for v in range(2) for w in range(half)]
+        for v in range(2) for q in range(C) for w in range(half)]
     receivers = [(z, r, side * half + w) for z in range(R) for w in range(half)]
     hops = [k for n in range(H // 2, 0, -1) for k in (n, R - n)]
     hops = list(dict.fromkeys(hops))
@@ -95,10 +101,11 @@
     fill = pltpu.make_async_copy(table, codes, table_sem)
     fill.start()
     p[T * RB] = jnp.zeros((BS, LANES), jnp.bfloat16)
-    fill.wait()
     panels = others(receivers)
     pl.semaphore_wait(
         barrier, len(hops) + Y * D + others(turned) + jnp.where(source, panels, 0))
+
+    fill.wait()
 
     left = lax.broadcasted_iota(jnp.int32, (BS, LANES), 1) < BS
 
@@ -115,7 +122,7 @@
 
     def panel_copy(q, w, v, did):
         return remote(
-            panel.at[q, w], block_of(x1, q * PB + d), scat_send.at[q, w, v], in1.at[v], did)
+            panel.at[q, w], block_at(x1, v * H, d), scat_send.at[q, w, v], in1.at[v], did)
 
     @pl.when(source)
     def _():
@@ -129,71 +136,102 @@
             @pl.when(is_self(s[-1]))
             def _(s=s):
                 pltpu.make_async_copy(
-                    panel.at[s[0], s[1]], block_of(x1, s[0] * PB + d), in1.at[s[2]]).start()
+                    panel.at[s[0], s[1]], block_at(x1, s[2] * H, d), in1.at[s[2]]).start()
 
             @pl.when(jnp.logical_not(is_self(s[-1])))
             def _(s=s):
                 panel_copy(*s).start()
 
+    starts = []
+    for q in range(R):
+        k = lax.rem(q - r + R, R)
+        starts.append(sum(jnp.where(k == key, n * PR, 0) for key, n in spot.items()))
+
     def densify(i, _):
         rows = pl.ds(pl.multiple_of(i * BS, BS), BS)
         for j in range(T):
-            dense[rows, j * LANES:(j + 1) * LANES] = placed(i, j)
+            q, within = j * R // T, j % (T // R) * LANES
+            at = pl.ds(pl.multiple_of(starts[q] + within, LANES), LANES)
+            dense[rows, at] = placed(i, j)
         return 0
 
     lax.fori_loop(0, RB, densify, 0)
+
+    def partial(x, begin, end):
+        def add(n, _):
+            rows = pl.ds(pl.multiple_of(n * 2 * PR, 2 * PR), 2 * PR)
+            term = jnp.dot(
+                dense[rows, begin:end], x[begin:end, :], preferred_element_type=jnp.float32)
+            part[rows, :] = term if begin == 0 else part[rows, :] + term
+            return 0
+
+        lax.fori_loop(0, C // 2, add, 0)
 
     def spread(x, arrived, sends, recvs):
         def copy(v, k):
-            at = piece_of(x, lax.rem(r + v * H, R))
-            return remote(at, at, sends.at[v, k], recvs.at[v, k], (lax.rem(r + k, R), c, d))
+            return remote(
+                piece_at(x, v * H), piece_at(x, v * H - k), sends.at[v, k], recvs.at[v, k],
+                (lax.rem(r + k, R), c, d))
 
         moves = [(v, k) for v in range(2) for k in hops if v == 0 or 2 * min(k, R - k) < H]
         for v in range(2):
-            at = piece_of(x, lax.rem(r + v * H, R))
+            at = piece_at(x, v * H)
             pltpu.make_async_copy(at, at, arrived.at[v]).wait()
             for move in moves:
                 if move[0] == v:
                     copy(*move).start()
+        partial(x, 0, cut1)
+        if cut2 > cut1:
+            for move in moves:
+                if (move[0] * H - move[1]) % R in near:
+                    copy(*move).wait_recv()
+            partial(x, cut1, cut2)
         for move in moves:
-            copy(*move).wait_recv()
+            if (move[0] * H - move[1]) % R in far:
+                copy(*move).wait_recv()
         return [copy(*move) for move in moves]
 
+    def rows_of(q):
+        return pl.ds(pl.multiple_of(q * PR, PR), PR)
+
     def product(x, q):
-        rows = pl.ds(pl.multiple_of(q * PR, PR), PR)
-        part[q] = jnp.dot(dense[rows, :], x[...], preferred_element_type=jnp.float32)
-
-    def coded(value, ref):
-        n = value.shape[0]
-        top = jnp.maximum(jnp.max(jnp.abs(value), axis=0, keepdims=True), 1e-30)
+        total = part[rows_of(q), :]
+        if far:
+            total = total + jnp.dot(
+                dense[rows_of(q), cut2:], x[cut2:, :], preferred_element_type=jnp.float32)
+        return total
+
+    def code(value, ref):
+        n = value.shape[1]
+        top = jnp.maximum(jnp.max(jnp.abs(value), axis=1, keepdims=True), 1e-30)
         level = jnp.ceil(jnp.log2(top) * 16.0) + 1.0
         scaled = jnp.round(value * (jnp.exp2(level * -0.0625) * 32000.0))
-        ref[0:n, :] = scaled.astype(jnp.int32).astype(jnp.int16)
-        ref[n:n + 16, :] = jnp.broadcast_to(
-            level, (16, LANES)).astype(jnp.int32).astype(jnp.int16)
-
-    def decoded(ref, n):
-        level = ref[n:n + 16, :].astype(jnp.int32).astype(jnp.float32)[0:1, :]
+        ref[:, 0:n, :] = scaled.astype(jnp.int32).astype(jnp.int16)
+        ref[:, n:n + 16, :] = jnp.broadcast_to(
+            level, (value.shape[0], 16, LANES)).astype(jnp.int32).astype(jnp.int16)
+
+    def decode(ref, n):
+        level = ref[:, n:n + 16, :].astype(jnp.int32).astype(jnp.float32)[:, 0:1, :]
         scale = jnp.exp2(level * 0.0625) * (1.0 / 32000.0)
-        return ref[0:n, :].astype(jnp.int32).astype(jnp.float32) * scale
-
-    far = sorted(range(1, Y), key=lambda k: -min(k, Y - k)) + [0]
+        return ref[:, 0:n, :].astype(jnp.int32).astype(jnp.float32) * scale
+
+    turns = sorted(range(1, Y), key=lambda k: -min(k, Y - k)) + [0]
 
     def to_sibling(x, k, buffer, sends, recvs):
         m = lax.rem(y + k, Y)
         q = 2 * m + 1 - core
-        return q, remote(part.at[q], buffer.at[k], sends.at[k], recvs.at[k], sibling)
+        return q, remote(part.at[rows_of(q)], buffer.at[k], sends.at[k], recvs.at[k], sibling)
 
     def with_sibling(x, buffer, sends, recvs, then):
-        for k in far:
+        for k in turns:
             q, copy = to_sibling(x, k, buffer, sends, recvs)
-            product(x, q)
+            part[rows_of(q), :] = product(x, q)
             copy.start()
-        for k in far:
+        for k in turns:
             q = 2 * lax.rem(y + k, Y) + core
-            product(x, q)
+            value = product(x, q)
             to_sibling(x, k, buffer, sends, recvs)[1].wait_recv()
-            then(k, q, part[q] + buffer[k])
+            then(k, q, value + buffer[k])
 
     sent1 = spread(x1, in1, ag1_send, ag1_recv)
 
@@ -203,7 +241,7 @@
 
     def send1(k, q, value):
         if k:
-            coded(value, sent.at[k])
+            code(value[None], sent.at[pl.ds(k, 1)])
             reduce1(k).start()
         else:
             square[...] = value
@@ -212,17 +250,17 @@
     total = square[...]
     for k in range(1, Y):
         reduce1(k).wait_recv()
-        total = total + decoded(recv.at[k], PR)
+        total = total + decode(recv.at[pl.ds(k, 1)], PR)[0]
     square[...] = total
     rounded[...] = total.astype(jnp.bfloat16)
 
     def turn(v):
-        return remote(rounded, piece_of(x2, c), turn_send.at[v], in2.at[v], turned[v])
+        return remote(rounded, piece_at(x2, v * H), turn_send.at[v], in2.at[v], turned[v])
 
     for v in range(2):
         @pl.when(is_self(turned[v]))
         def _(v=v):
-            pltpu.make_async_copy(rounded, piece_of(x2, c), in2.at[v]).start()
+            pltpu.make_async_copy(rounded, piece_at(x2, v * H), in2.at[v]).start()
 
         @pl.when(jnp.logical_not(is_self(turned[v])))
         def _(v=v):
@@ -234,40 +272,39 @@
             square.at[pl.ds(pl.multiple_of(to * BS, BS), BS)], owned.at[d],
             sq_send.at[e], sq_recv.at[e], (r, c, to))
 
-    sent2 = spread(x2, in2, ag2_send, ag2_recv)
-    for e in range(1, D):
-        give(e).start()
     for k in range(Y):
         to_sibling(x1, k, core1, core1_send, core1_recv)[1].wait_send()
         if k:
             reduce1(k).wait_send()
+    sent2 = spread(x2, in2, ag2_send, ag2_recv)
+    for e in range(1, D):
+        give(e).start()
 
     def cube(k, e):
         q, to = 2 * lax.rem(y + k, Y) + core, lax.rem(d + e, D)
         return remote(
-            shares.at[k * D + e], cubes.at[y * D + d],
+            shares.at[k, to], cubes.at[y * D + d],
             cu_send.at[k * D + e], cu_recv, (r, q, to))
 
     def send2(k, q, value):
-        part[q] = value
+        code(value.reshape(D, BS, LANES), shares.at[k])
         for e in sorted(range(D), key=lambda e: -min(e, D - e)):
-            to = pl.ds(pl.multiple_of(lax.rem(d + e, D) * BS, BS), BS)
-            coded(part[q, to, :], shares.at[k * D + e])
             if k or e:
                 cube(k, e).start()
             else:
-                pltpu.make_async_copy(shares.at[0], cubes.at[y * D + d], cu_recv).start()
+                pltpu.make_async_copy(shares.at[0, d], cubes.at[y * D + d], cu_recv).start()
 
     with_sibling(x2, core2, core2_send, core2_recv, send2)
     for e in range(1, D):
         give(e).wait_recv()
     pltpu.make_async_copy(cubes, cubes, cu_recv).wait()
-    own = square[pl.ds(pl.multiple_of(d * BS, BS), BS), :]
+    mine = square[pl.ds(pl.multiple_of(d * BS, BS), BS), :]
+    sums = decode(cubes.at[pl.ds(0, D)], BS)
+    for m in range(1, Y):
+        sums = sums + decode(cubes.at[pl.ds(m * D, D)], BS)
     for e in range(D):
-        total = decoded(cubes.at[e], BS)
-        for m in range(1, Y):
-            total = total + decoded(cubes.at[m * D + e], BS)
-        out[:, e * LANES:(e + 1) * LANES] = 3.0 * jnp.where(d == e, own, owned[e]) - 2.0 * total
+        total = sums[e]
+        out[:, e * LANES:(e + 1) * LANES] = 3.0 * jnp.where(d == e, mine, owned[e]) - 2.0 * total
 
     @pl.when(source)
     def _():
@@ -313,14 +350,14 @@
             pltpu.VMEM((C, D // 2, BS, LANES), bf),
             pltpu.VMEM((K, LANES), bf),
             pltpu.VMEM((K, LANES), bf),
-            pltpu.VMEM((C, PR, LANES), f32),
+            pltpu.VMEM((K, LANES), f32),
             pltpu.VMEM((Y, PR, LANES), f32),
             pltpu.VMEM((Y, PR, LANES), f32),
             pltpu.VMEM((Y, PR + 16, LANES), jnp.int16),
             pltpu.VMEM((Y, PR + 16, LANES), jnp.int16),
             pltpu.VMEM((PR, LANES), f32),
             pltpu.VMEM((PR, LANES), bf),
-            pltpu.VMEM((Y * D, BS + 16, LANES), jnp.int16),
+            pltpu.VMEM((Y, D, BS + 16, LANES), jnp.int16),
             pltpu.VMEM((Y * D, BS + 16, LANES), jnp.int16),
             pltpu.VMEM((D, BS, LANES), f32),
             dma, dma((T,)), dma((C, D // 2, 2)), dma((2,)), dma((2, R)), dma((2, R)),
@@ -331,8 +368,8 @@
         compiler_params=pltpu.CompilerParams(
             collective_id=0, has_side_effects=True, vmem_limit_bytes=48 << 20),
     )(p_blocks, p_cols)
-    shaped = rows.reshape(1, BS, WB, BS) * out_mask.astype(f32)[:, None, :, None]
-    return shaped.reshape(1, BS, WB * BS)
+    kept = jnp.repeat(out_mask.astype(f32), BS, axis=1)
+    return (rows * kept).reshape(1, BS, WB * BS)
 
 
 def solution(mesh):

time: 61.4 us -> 59.7 us (0.972)
  Pallas kernels: 59.1 us -> 57.3 us
    pallas_call x1, Pallas kernels: 59.1 us -> 57.3 us  [body(): pl.pallas_call(functools.partial(kernel, R, C, D, RB, BS), out_shape=jax....]
    mul x2 -> x0, other arithmetic: 1.33 us -> none  [body(): rows.reshape(1, BS, WB, BS) * out_mask.astype(f32)[:, None, :, None]]
    reshape x0 -> x1, other arithmetic: none -> 0.67 us  [body(): return (rows * kept).reshape(1, BS, WB * BS)]
    convert_element_type x0 -> x1, other arithmetic: none -> 0.66 us  [body(): kept = jnp.repeat(out_mask.astype(f32), BS, axis=1)]
where the time goes in v4:
time: 59.7 us; the launch traced here: 59.5 us
  Pallas kernels  57.3 us (96%)
  other arithmetic  1.33 us (2%)
  local copies, waits for them, and re-layouts  0.87 us (1%)
    pallas_call x1, Pallas kernels, body(): pl.pallas_call(functools.partial(kernel, R, C, D, RB, BS), out_shape=jax....  57.3 us

profile of v4, /device:TPU:1, one launch (start us, length us, event | category | flops | bytes accessed | tf_op | source)
XLA Modules:
  0.0 59.5 jit_solution(16965476210498877646)
XLA Ops:
  0.0 0.7 %convert_bitcast_fusion = f32[8]{0:T(128)S(1)} fusion(s32[1,8]{1,0:T(1,128)} %param.5), kind=kLoop, calls=%fused_computation.1 | loop fusion | flops 8 | bytes 64 | tf_op jit(solution)/shard_map/convert_element_type | solution.py:371
  0.7 0.1 broadcast_in_dim.5
  0.7 0.1 broadcast_in_dim.6
  0.8 0.0 copy-start
  0.8 0.7 %copy-done = s32[32,32]{1,0:T(8,128)S(1)} copy-done((s32[32,32]{1,0:T(8,128)S(1)}, s32[32,32]{1,0:T(8,128)}, u32[]{:S(2)}) %copy-start) | copy-done | bytes 4120
  1.5 57.3 %shard_map.37 = f32[64,512]{1,0:T(8,128)S(1)} custom-call(bf16[32,64,2048]{2,1,0:T(8,128)(2,1)} %p_hbm.1, s32[32,32]{1,0:T(8,128)S(1)} %copy-done), custom_call_target="tpu_custom_call" | custom-call | tf_op jit(solution)/shard_map/pallas_call | solution.py:340
  58.9 0.7 %multiply_bitcast_fusion = f32[1,64,512]{2,1,0:T(8,128)} fusion(f32[64,512]{1,0:T(8,128)S(1)} %shard_map.37, f32[512]{0:T(512)S(1)} %broadcast_in_dim.6), kind=kLoop, calls=%fused_computation | loop fusion | flops 32768 | bytes 264192 | tf_op jit(solution)/shard_map/reshape | solution.py:372
Async XLA Ops:
  0.8 0.7 %copy-start = (s32[32,32]{1,0:T(8,128)S(1)}, s32[32,32]{1,0:T(8,128)}, u32[]{:S(2)}) copy-start(s32[32,32]{1,0:T(8,128)} %cols.1) | copy-start | bytes 12292

commit v5 on v4

--- a/solution.py
+++ b/solution.py
@@ -55,8 +55,8 @@
             p_hbm.at[:, :, pl.ds(t * LANES, LANES)], p.at[pl.ds(t * RB, RB)], load_sem.at[t])
 
     scatter = [
-        (q, w, v, ((q + v * H) % R, r, side * half + w))
-        for v in range(2) for q in range(C) for w in range(half)]
+        (lax.rem(r + k + R - v * H, R), w, v, k, (lax.rem(r + k, R), r, side * half + w))
+        for v in range(2) for k in range(R) for w in range(half)]
     receivers = [(z, r, side * half + w) for z in range(R) for w in range(half)]
     hops = [k for n in range(H // 2, 0, -1) for k in (n, R - n)]
     hops = list(dict.fromkeys(hops))
@@ -120,9 +120,9 @@
     for t in range(T):
         load(t).wait()
 
-    def panel_copy(q, w, v, did):
+    def panel_copy(q, w, v, k, did):
         return remote(
-            panel.at[q, w], block_at(x1, v * H, d), scat_send.at[q, w, v], in1.at[v], did)
+            panel.at[q, w], block_at(x1, v * H, d), scat_send.at[k, w, v], in1.at[v], did)
 
     @pl.when(source)
     def _():
@@ -133,6 +133,10 @@
 
         lax.fori_loop(0, C, extract, 0)
         for s in scatter:
+            if s[3]:
+                panel_copy(*s).start()
+                continue
+
             @pl.when(is_self(s[-1]))
             def _(s=s):
                 pltpu.make_async_copy(
@@ -309,6 +313,10 @@
     @pl.when(source)
     def _():
         for s in scatter:
+            if s[3]:
+                panel_copy(*s).wait_send()
+                continue
+
             @pl.when(jnp.logical_not(is_self(s[-1])))
             def _(s=s):
                 panel_copy(*s).wait_send()

time: 59.7 us -> 59.5 us (level)
  no operation moved by 1% of the time
where the time goes in v5:
time: 59.5 us; the launch traced here: 59.3 us
  Pallas kernels  57.1 us (96%)
  other arithmetic  1.33 us (2%)
  local copies, waits for them, and re-layouts  0.87 us (1%)
    pallas_call x1, Pallas kernels, body(): pl.pallas_call(functools.partial(kernel, R, C, D, RB, BS), out_shape=jax....  57.1 us

profile of v5, /device:TPU:1, one launch (start us, length us, event | category | flops | bytes accessed | tf_op | source)
XLA Modules:
  0.0 59.3 jit_solution(4625453092854969389)
XLA Ops:
  0.0 0.7 %convert_bitcast_fusion = f32[8]{0:T(128)S(1)} fusion(s32[1,8]{1,0:T(1,128)} %param.5), kind=kLoop, calls=%fused_computation.1 | loop fusion | flops 8 | bytes 64 | tf_op jit(solution)/shard_map/convert_element_type | solution.py:379
  0.7 0.1 broadcast_in_dim.5
  0.7 0.1 broadcast_in_dim.6
  0.8 0.0 copy-start
  0.8 0.7 %copy-done = s32[32,32]{1,0:T(8,128)S(1)} copy-done((s32[32,32]{1,0:T(8,128)S(1)}, s32[32,32]{1,0:T(8,128)}, u32[]{:S(2)}) %copy-start) | copy-done | bytes 4120
  1.5 57.1 %shard_map.37 = f32[64,512]{1,0:T(8,128)S(1)} custom-call(bf16[32,64,2048]{2,1,0:T(8,128)(2,1)} %p_hbm.1, s32[32,32]{1,0:T(8,128)S(1)} %copy-done), custom_call_target="tpu_custom_call" | custom-call | tf_op jit(solution)/shard_map/pallas_call | solution.py:348
  58.6 0.7 %multiply_bitcast_fusion = f32[1,64,512]{2,1,0:T(8,128)} fusion(f32[64,512]{1,0:T(8,128)S(1)} %shard_map.37, f32[512]{0:T(512)S(1)} %broadcast_in_dim.6), kind=kLoop, calls=%fused_computation | loop fusion | flops 32768 | bytes 264192 | tf_op jit(solution)/shard_map/reshape | solution.py:380
Async XLA Ops:
  0.8 0.7 %copy-start = (s32[32,32]{1,0:T(8,128)S(1)}, s32[32,32]{1,0:T(8,128)}, u32[]{:S(2)}) copy-start(s32[32,32]{1,0:T(8,128)} %cols.1) | copy-start | bytes 12292

commit v6 on v4

--- a/solution.py
+++ b/solution.py
@@ -39,10 +39,9 @@
         return (did[0] == r) & (did[1] == c) & (did[2] == d)
 
     own = list(dict.fromkeys([0, H]))
-    far = [k for k in range(R) if k not in own]
-    near = [k for k in range(R) if k not in own + far]
-    spot = {k: n for n, k in enumerate(own + near + far)}
-    cut1, cut2 = len(own) * PR, len(own + near) * PR
+    far = sorted((k for k in range(R) if k not in own), key=lambda k: k % 2)
+    spot = {k: n for n, k in enumerate(own + far)}
+    evens = list(range(0, R, 2))
 
     def piece_at(x, k):
         return x.at[spot[k % R] * PR:(spot[k % R] + 1) * PR]
@@ -60,7 +59,7 @@
     receivers = [(z, r, side * half + w) for z in range(R) for w in range(half)]
     hops = [k for n in range(H // 2, 0, -1) for k in (n, R - n)]
     hops = list(dict.fromkeys(hops))
-    turned = [(lax.rem(c + v * H, R), r, d) for v in range(2)]
+    turned = [(lax.rem(c + o, R), r, d) for o in evens]
 
     barrier = pltpu.get_barrier_semaphore()
 
@@ -74,8 +73,8 @@
 
     for e in range(D):
         hello_other((c, (d // half) * Y, lax.rem(d + e, D)))
-    for v in range(2):
-        hello_other((c, lax.rem(r + v * H, R), d))
+    for o in evens:
+        hello_other((c, lax.rem(r + R - o, R), d))
     for k in hops:
         hello((lax.rem(r + k, R), c, d))
     hello(sibling)
@@ -167,39 +166,30 @@
 
         lax.fori_loop(0, C // 2, add, 0)
 
-    def spread(x, arrived, sends, recvs):
-        def copy(v, k):
+    def spread(x, held, moves, arrived, sends, recvs):
+        def copy(n):
+            o, k = moves[n]
             return remote(
-                piece_at(x, v * H), piece_at(x, v * H - k), sends.at[v, k], recvs.at[v, k],
+                piece_at(x, o), piece_at(x, o - k), sends.at[n], recvs.at[n],
                 (lax.rem(r + k, R), c, d))
 
-        moves = [(v, k) for v in range(2) for k in hops if v == 0 or 2 * min(k, R - k) < H]
-        for v in range(2):
-            at = piece_at(x, v * H)
+        for v, o in enumerate(held):
+            at = piece_at(x, o)
             pltpu.make_async_copy(at, at, arrived.at[v]).wait()
-            for move in moves:
-                if move[0] == v:
-                    copy(*move).start()
-        partial(x, 0, cut1)
-        if cut2 > cut1:
-            for move in moves:
-                if (move[0] * H - move[1]) % R in near:
-                    copy(*move).wait_recv()
-            partial(x, cut1, cut2)
-        for move in moves:
-            if (move[0] * H - move[1]) % R in far:
-                copy(*move).wait_recv()
-        return [copy(*move) for move in moves]
+            for n, move in enumerate(moves):
+                if move[0] == o:
+                    copy(n).start()
+        partial(x, 0, len(held) * PR)
+        for n in range(len(moves)):
+            copy(n).wait_recv()
+        return [copy(n) for n in range(len(moves))]
 
     def rows_of(q):
         return pl.ds(pl.multiple_of(q * PR, PR), PR)
 
-    def product(x, q):
-        total = part[rows_of(q), :]
-        if far:
-            total = total + jnp.dot(
-                dense[rows_of(q), cut2:], x[cut2:, :], preferred_element_type=jnp.float32)
-        return total
+    def product(x, begin, q):
+        return part[rows_of(q), :] + jnp.dot(
+            dense[rows_of(q), begin:], x[begin:, :], preferred_element_type=jnp.float32)
 
     def code(value, ref):
         n = value.shape[1]
@@ -222,18 +212,20 @@
         q = 2 * m + 1 - core
         return q, remote(part.at[rows_of(q)], buffer.at[k], sends.at[k], recvs.at[k], sibling)
 
-    def with_sibling(x, buffer, sends, recvs, then):
+    def with_sibling(x, begin, buffer, sends, recvs, then):
         for k in turns:
             q, copy = to_sibling(x, k, buffer, sends, recvs)
-            part[rows_of(q), :] = product(x, q)
+            part[rows_of(q), :] = product(x, begin, q)
             copy.start()
         for k in turns:
             q = 2 * lax.rem(y + k, Y) + core
-            value = product(x, q)
+            value = product(x, begin, q)
             to_sibling(x, k, buffer, sends, recvs)[1].wait_recv()
             then(k, q, value + buffer[k])
 
-    sent1 = spread(x1, in1, ag1_send, ag1_recv)
+    moves1 = [(0, k) for k in hops] + [(H, k) for k in hops if 2 * min(k, R - k) < H]
+    moves2 = [(0, 1), (0, R - 1), (2, R - 1), (R - 2, 1)]
+    sent1 = spread(x1, own, moves1, in1, ag1_send, ag1_recv)
 
     def reduce1(k):
         q = 2 * lax.rem(y + k, Y) + core
@@ -246,7 +238,7 @@
         else:
             square[...] = value
 
-    with_sibling(x1, core1, core1_send, core1_recv, send1)
+    with_sibling(x1, 2 * PR, core1, core1_send, core1_recv, send1)
     total = square[...]
     for k in range(1, Y):
         reduce1(k).wait_recv()
@@ -255,12 +247,12 @@
     rounded[...] = total.astype(jnp.bfloat16)
 
     def turn(v):
-        return remote(rounded, piece_at(x2, v * H), turn_send.at[v], in2.at[v], turned[v])
-
-    for v in range(2):
+        return remote(rounded, piece_at(x2, -2 * v), turn_send.at[v], in2.at[-v % len(evens)], turned[v])
+
+    for v in range(len(evens)):
         @pl.when(is_self(turned[v]))
         def _(v=v):
-            pltpu.make_async_copy(rounded, piece_at(x2, v * H), in2.at[v]).start()
+            pltpu.make_async_copy(rounded, piece_at(x2, -2 * v), in2.at[-v % len(evens)]).start()
 
         @pl.when(jnp.logical_not(is_self(turned[v])))
         def _(v=v):
@@ -276,7 +268,7 @@
         to_sibling(x1, k, core1, core1_send, core1_recv)[1].wait_send()
         if k:
             reduce1(k).wait_send()
-    sent2 = spread(x2, in2, ag2_send, ag2_recv)
+    sent2 = spread(x2, evens, moves2, in2, ag2_send, ag2_recv)
     for e in range(1, D):
         give(e).start()
 
@@ -294,7 +286,7 @@
             else:
                 pltpu.make_async_copy(shares.at[0, d], cubes.at[y * D + d], cu_recv).start()
 
-    with_sibling(x2, core2, core2_send, core2_recv, send2)
+    with_sibling(x2, len(evens) * PR, core2, core2_send, core2_recv, send2)
     for e in range(1, D):
         give(e).wait_recv()
     pltpu.make_async_copy(cubes, cubes, cu_recv).wait()
@@ -315,7 +307,7 @@
 
     for copy in sent1 + sent2:
         copy.wait_send()
-    for v in range(2):
+    for v in range(len(evens)):
         @pl.when(jnp.logical_not(is_self(turned[v])))
         def _(v=v):
             turn(v).wait_send()
@@ -360,9 +352,9 @@
             pltpu.VMEM((Y, D, BS + 16, LANES), jnp.int16),
             pltpu.VMEM((Y * D, BS + 16, LANES), jnp.int16),
             pltpu.VMEM((D, BS, LANES), f32),
-            dma, dma((T,)), dma((C, D // 2, 2)), dma((2,)), dma((2, R)), dma((2, R)),
+            dma, dma((T,)), dma((C, D // 2, 2)), dma((2,)), dma((R,)), dma((R,)),
             dma((Y,)), dma((Y,)), dma((Y,)), dma((Y,)),
-            dma((2,)), dma((2,)), dma((2, R)), dma((2, R)), dma((D,)), dma((D,)),
+            dma((R // 2,)), dma((R // 2,)), dma((R,)), dma((R,)), dma((D,)), dma((D,)),
             dma((Y,)), dma((Y,)), dma((Y * D,)), dma,
         ],
         compiler_params=pltpu.CompilerParams(

time: 59.7 us -> 58.7 us (0.983)
  Pallas kernels: 57.3 us -> 56.3 us
    pallas_call x1, Pallas kernels: 57.3 us -> 56.3 us  [body(): pl.pallas_call(functools.partial(kernel, R, C, D, RB, BS), out_shape=jax....]
where the time goes in v6:
time: 58.7 us; the launch traced here: 58.5 us
  Pallas kernels  56.3 us (96%)
  other arithmetic  1.33 us (2%)
  local copies, waits for them, and re-layouts  0.87 us (1%)
    pallas_call x1, Pallas kernels, body(): pl.pallas_call(functools.partial(kernel, R, C, D, RB, BS), out_shape=jax....  56.3 us

profile of v6, /device:TPU:1, one launch (start us, length us, event | category | flops | bytes accessed | tf_op | source)
XLA Modules:
  0.0 58.5 jit_solution(17699885997212644153)
XLA Ops:
  0.0 0.7 %convert_bitcast_fusion = f32[8]{0:T(128)S(1)} fusion(s32[1,8]{1,0:T(1,128)} %param.5), kind=kLoop, calls=%fused_computation.1 | loop fusion | flops 8 | bytes 64 | tf_op jit(solution)/shard_map/convert_element_type | solution.py:363
  0.7 0.1 broadcast_in_dim.5
  0.7 0.1 broadcast_in_dim.6
  0.8 0.0 copy-start
  0.8 0.7 %copy-done = s32[32,32]{1,0:T(8,128)S(1)} copy-done((s32[32,32]{1,0:T(8,128)S(1)}, s32[32,32]{1,0:T(8,128)}, u32[]{:S(2)}) %copy-start) | copy-done | bytes 4120
  1.5 56.3 %shard_map.37 = f32[64,512]{1,0:T(8,128)S(1)} custom-call(bf16[32,64,2048]{2,1,0:T(8,128)(2,1)} %p_hbm.1, s32[32,32]{1,0:T(8,128)S(1)} %copy-done), custom_call_target="tpu_custom_call" | custom-call | tf_op jit(solution)/shard_map/pallas_call | solution.py:332
  57.9 0.7 %multiply_bitcast_fusion = f32[1,64,512]{2,1,0:T(8,128)} fusion(f32[64,512]{1,0:T(8,128)S(1)} %shard_map.37, f32[512]{0:T(512)S(1)} %broadcast_in_dim.6), kind=kLoop, calls=%fused_computation | loop fusion | flops 32768 | bytes 264192 | tf_op jit(solution)/shard_map/reshape | solution.py:364
Async XLA Ops:
  0.8 0.7 %copy-start = (s32[32,32]{1,0:T(8,128)S(1)}, s32[32,32]{1,0:T(8,128)}, u32[]{:S(2)}) copy-start(s32[32,32]{1,0:T(8,128)} %cols.1) | copy-start | bytes 12292

commit v7 on v6

--- a/solution.py
+++ b/solution.py
@@ -173,7 +173,8 @@
                 piece_at(x, o), piece_at(x, o - k), sends.at[n], recvs.at[n],
                 (lax.rem(r + k, R), c, d))
 
-        for v, o in enumerate(held):
+        sent_on = [o for o, _ in moves]
+        for v, o in sorted(enumerate(held), key=lambda held: held[1] not in sent_on):
             at = piece_at(x, o)
             pltpu.make_async_copy(at, at, arrived.at[v]).wait()
             for n, move in enumerate(moves):
@@ -249,7 +250,7 @@
     def turn(v):
         return remote(rounded, piece_at(x2, -2 * v), turn_send.at[v], in2.at[-v % len(evens)], turned[v])
 
-    for v in range(len(evens)):
+    for v in sorted(range(len(evens)), key=lambda v: 2 * v == H):
         @pl.when(is_self(turned[v]))
         def _(v=v):
             pltpu.make_async_copy(rounded, piece_at(x2, -2 * v), in2.at[-v % len(evens)]).start()

time: 58.7 us -> 58.7 us (level)
  no operation moved by 1% of the time
where the time goes in v7:
time: 58.7 us; the launch traced here: 58.5 us
  Pallas kernels  56.3 us (96%)
  other arithmetic  1.33 us (2%)
  local copies, waits for them, and re-layouts  0.87 us (1%)
    pallas_call x1, Pallas kernels, body(): pl.pallas_call(functools.partial(kernel, R, C, D, RB, BS), out_shape=jax....  56.3 us

profile of v7, /device:TPU:1, one launch (start us, length us, event | category | flops | bytes accessed | tf_op | source)
XLA Modules:
  0.0 58.5 jit_solution(6062307531172261641)
XLA Ops:
  0.0 0.7 %convert_bitcast_fusion = f32[8]{0:T(128)S(1)} fusion(s32[1,8]{1,0:T(1,128)} %param.5), kind=kLoop, calls=%fused_computation.1 | loop fusion | flops 8 | bytes 64 | tf_op jit(solution)/shard_map/convert_element_type | solution.py:364
  0.7 0.1 broadcast_in_dim.5
  0.7 0.1 broadcast_in_dim.6
  0.8 0.0 copy-start
  0.8 0.7 %copy-done = s32[32,32]{1,0:T(8,128)S(1)} copy-done((s32[32,32]{1,0:T(8,128)S(1)}, s32[32,32]{1,0:T(8,128)}, u32[]{:S(2)}) %copy-start) | copy-done | bytes 4120
  1.5 56.3 %shard_map.37 = f32[64,512]{1,0:T(8,128)S(1)} custom-call(bf16[32,64,2048]{2,1,0:T(8,128)(2,1)} %p_hbm.1, s32[32,32]{1,0:T(8,128)S(1)} %copy-done), custom_call_target="tpu_custom_call" | custom-call | tf_op jit(solution)/shard_map/pallas_call | solution.py:333
  57.9 0.7 %multiply_bitcast_fusion = f32[1,64,512]{2,1,0:T(8,128)} fusion(f32[64,512]{1,0:T(8,128)S(1)} %shard_map.37, f32[512]{0:T(512)S(1)} %broadcast_in_dim.6), kind=kLoop, calls=%fused_computation | loop fusion | flops 32768 | bytes 264192 | tf_op jit(solution)/shard_map/reshape | solution.py:365
Async XLA Ops:
  0.8 0.7 %copy-start = (s32[32,32]{1,0:T(8,128)S(1)}, s32[32,32]{1,0:T(8,128)}, u32[]{:S(2)}) copy-start(s32[32,32]{1,0:T(8,128)} %cols.1) | copy-start | bytes 12292
